TPU v7x, 32 devices: a whole 2x2x4 slice. The times are simulated.
32 devices in a mesh: pair: 2 (over y), section: 4 (over z), dp: 4 (over x, core).
Axes of the slice: x: 2, y: 2, z: 4, core: 2. Of those that a mesh axis runs over, the one named last changes fastest.
Arguments:
- grads: float32 [8, 4, 8, 7168], P(('section', 'pair'), 'dp'), parts along dimension 0, may hold values from -6 to 6
- master: float32 [32, 7168], P(('section', 'pair', 'dp')), parts along dimension 0, may hold values from -6 to 6
- moment: float32 [32, 7168], P(('section', 'pair', 'dp')), parts along dimension 0, may hold values from -12 to 12
- second: float32 [32, 7168], P(('section', 'pair', 'dp')), parts along dimension 0, may hold values from 0.5 to 50
- step: int32 [4], P('section'), parts along dimension 0, may hold values from 1 to 8
Outputs:
- new_master: float32 [32, 7168], P(('section', 'pair', 'dp')), parts along dimension 0
- new_moment: float32 [32, 7168], P(('section', 'pair', 'dp')), parts along dimension 0
- new_second: float32 [32, 7168], P(('section', 'pair', 'dp')), parts along dimension 0
- params: bfloat16 [32, 7168], P('section'), parts along dimension 0
There are 4 independent parts, one for each index of `section`. A program takes and returns all parts, laid end to end along the dimension named above; each array names one. Nothing has to cross between parts.
All inputs are finite; a program needn't handle non-finite values.
Results may differ from a plain program's by a relative error of at most 0.0004.
Values may be sent and summed in bfloat16 or wider, within the bound.
No kernel may reach another device: no remote copies, remote signals or barrier semaphores. Data moves between devices by JAX's collectives and lax.ppermute only.
A program may use at most 64 MiB of HBM per device.

v0:
```python
import jax
import jax.numpy as jnp
from jax import lax
from jax.sharding import PartitionSpec as P


def per_device(grads, master, moment, second, step):
    local = grads.reshape(grads.shape[2], grads.shape[3])
    total = lax.psum_scatter(local, ("pair", "dp"), scatter_dimension=0, tiled=True)
    new_moment = 0.9 * moment + 0.1 * total
    new_second = 0.95 * second + 0.05 * total * total
    count = step[0].astype(jnp.float32)
    first_fix = 1.0 - jnp.power(jnp.float32(0.9), count)
    second_fix = 1.0 - jnp.power(jnp.float32(0.95), count)
    update = new_moment / first_fix / (jnp.sqrt(new_second / second_fix) + 1e-08) + 0.1 * master
    new_master = master - 0.03 * update
    shard_params = new_master.astype(jnp.bfloat16)
    params = lax.all_gather(shard_params, ("pair", "dp"), axis=0, tiled=True)
    return (new_master, new_moment, new_second, params)


def solution(mesh):
    placed = (
        P(("section", "pair"), "dp", None, None),
        P(("section", "pair", "dp"), None),
        P(("section", "pair", "dp"), None),
        P(("section", "pair", "dp"), None),
        P("section"),
    )
    return jax.shard_map(
        per_device,
        mesh=mesh,
        in_specs=placed,
        out_specs=(
            P(("section", "pair", "dp"), None),
            P(("section", "pair", "dp"), None),
            P(("section", "pair", "dp"), None),
            P("section", None),
        ),
        check_vma=False,
    )
```

profile of v0, /device:TPU:0, one launch (start us, length us, event | category | flops | bytes accessed | tf_op | source)
XLA Modules:
  0.0 85.8 jit_solution(5662193489627483390)
XLA Ops:
  7.2 0.0 all-reduce.3.cloned.1.call-start
  7.2 0.0 copy-start.1
  7.2 0.0 copy-start.2
  7.2 0.7 all-reduce.3.cloned.1.call-update
  7.9 0.0 copy-start
  8.6 0.0 copy-start.3
  8.7 0.6 copy-done.3
  9.3 0.6 dynamic-slice
  9.9 56.0 %all-reduce.3.cloned.1.call-done = f32[8,7168]{1,0:T(8,128)} async-done(((f32[8,7168]{1,0:T(8,128)}), f32[8,7168]{1,0:T(8,128)}) %all-reduce.3.cloned.1.call-update) | async-done | bytes 229392
  65.9 0.0 copy-done.1
  65.9 0.0 copy-done.2
  65.9 0.0 copy-done
  65.9 2.3 %convert_bitcast_fusion = (bf16[1,1,7168]{2,1,0:T(2,128)(2,1)S(1)}, f32[1,7168]{1,0:T(1,128)}, f32[1,7168]{1,0:T(1,128)}, f32[1,7168]{1,0:T(1,128)}) fusion(f32[1,7168]{1,0:T(1,128)S(1)} %copy-done, f32[]{:T(128)} %bitcast.3, f32[]{:T(128)} %bitcast.2, f32[8,7168]{1,0:T(8,128)} %all-reduce.3.cloned.1.call-done, u32[]{:T(128)} %bitcast.1, ...), kind=kLoop, calls=%fused_computation.3 | loop fusion | flops 114688 | bytes 215052
  68.2 10.0 %all-gather = bf16[8,1,7168]{2,1,0:T(2,128)(2,1)S(1)} all-gather(bf16[1,1,7168]{2,1,0:T(2,128)(2,1)S(1)} %get-tuple-element.4), channel_id=1, replica_groups=mesh['pair'=2,'section'=4,'dp'=4] {'pair','dp'}, dimensions={0}, use_global_device_ids=true | all-gather | bytes 129024 | tf_op jit(solution)/shard_map/all_gather | solution.py:18
  78.3 0.7 copy.11
Async XLA Ops:
  7.2 58.7 %all-reduce.3.cloned.1.call-start = ((), (), s32[]{:S(2)}) async-start(), calls=%async_computation | async-start | bytes 458752
  7.2 58.7 %copy-start.1 = (f32[1,7168]{1,0:T(1,128)S(1)}, f32[1,7168]{1,0:T(1,128)}, u32[]{:S(2)}) copy-start(f32[1,7168]{1,0:T(1,128)} %param.8) | copy-start | bytes 86020
  7.2 58.7 %copy-start.2 = (f32[1,7168]{1,0:T(1,128)S(1)}, f32[1,7168]{1,0:T(1,128)}, u32[]{:S(2)}) copy-start(f32[1,7168]{1,0:T(1,128)} %param.7) | copy-start | bytes 86020
  7.9 58.0 %copy-start = (f32[1,7168]{1,0:T(1,128)S(1)}, f32[1,7168]{1,0:T(1,128)}, u32[]{:S(2)}) copy-start(f32[1,7168]{1,0:T(1,128)} %param.6) | copy-start | bytes 86020
  8.6 0.7 copy-start.3
Sparse Core Ops, SparseCore 0:
  11.1 54.7 all-reduce.2
where the time goes:
time: 86 us; the launch traced here: 85.8 us
  waiting for transfers between devices  56.7 us (66%)
  between operations  14.8 us (17%)
  blocking collectives  10 us (12%)
  other arithmetic  2.33 us (3%)
  local copies, waits for them, and re-layouts  1.93 us (2%)
    unnamed x2, waiting for transfers between devices  56.7 us
    all_gather x1, blocking collectives, per_device(): params = lax.all_gather(shard_params, ('pair', 'dp'), axis=0, tiled=True)  10 us
    unnamed x1, other arithmetic  2.33 us
    unnamed x10, local copies, waits for them, and re-layouts  1.93 us
  transfers between devices with their start and end apart: 1, of which 1 were waited for; matrix products, arithmetic and copies ran while one was open for 1% of the time, Pallas kernels for 0%

commit v1 on v0

--- a/solution.py
+++ b/solution.py
@@ -3,20 +3,71 @@
 from jax import lax
 from jax.sharding import PartitionSpec as P
 
+GROUP = ("pair", "dp")
 
-def per_device(grads, master, moment, second, step):
-    local = grads.reshape(grads.shape[2], grads.shape[3])
-    total = lax.psum_scatter(local, ("pair", "dp"), scatter_dimension=0, tiled=True)
+
+def swap(array, bit):
+    size = lax.axis_size(GROUP)
+    return lax.ppermute(array, GROUP, [(i, i ^ bit) for i in range(size)])
+
+
+def take(array, axis, index):
+    return lax.dynamic_slice_in_dim(array, index, 1, axis)
+
+
+def adam(total, master, moment, second, step):
     new_moment = 0.9 * moment + 0.1 * total
     new_second = 0.95 * second + 0.05 * total * total
     count = step[0].astype(jnp.float32)
     first_fix = 1.0 - jnp.power(jnp.float32(0.9), count)
     second_fix = 1.0 - jnp.power(jnp.float32(0.95), count)
     update = new_moment / first_fix / (jnp.sqrt(new_second / second_fix) + 1e-08) + 0.1 * master
-    new_master = master - 0.03 * update
-    shard_params = new_master.astype(jnp.bfloat16)
-    params = lax.all_gather(shard_params, ("pair", "dp"), axis=0, tiled=True)
-    return (new_master, new_moment, new_second, params)
+    return master - 0.03 * update, new_moment, new_second
+
+
+def in_order(first, mine, theirs):
+    return jnp.where(first, mine, theirs), jnp.where(first, theirs, mine)
+
+
+def per_device(grads, master, moment, second, step):
+    rows, width = grads.shape[2], grads.shape[3]
+    own = master.shape[0]
+    pairs, shards = lax.axis_size("pair"), lax.axis_size("dp")
+    pair, shard = lax.axis_index("pair"), lax.axis_index("dp")
+    half = shards
+
+    state = jnp.concatenate([master, moment, second], axis=0)
+    other_state = swap(state, half)
+
+    local = grads.reshape(rows, width)
+    local = (local + swap(local, 1)).reshape(pairs, shards, own, width)
+    bit, kept = 1, local.reshape(pairs, shards // 2, 2, own, width)
+    kept = take(kept, 2, shard & 1)[:, :, 0]
+    while kept.shape[1] > 1:
+        bit *= 2
+        split = kept.reshape(pairs, kept.shape[1] // 2, 2, own, width)
+        mine = jnp.where((shard & bit) != 0, 1, 0)
+        give = take(split, 2, 1 - mine)[:, :, 0]
+        kept = take(split, 2, mine)[:, :, 0] + swap(give, bit)
+    both = kept.reshape(pairs * own, width)
+    both = both + swap(both, half)
+
+    first = pair == 0
+    mine, theirs = jnp.where(first, both[:own], both[own:]), jnp.where(first, both[own:], both[:own])
+    new_master, new_moment, new_second = adam(mine, master, moment, second, step)
+    other = other_state.reshape(3, own, width)
+    other_master, _, _ = adam(theirs, other[0], other[1], other[2], step)
+
+    params = [p.astype(jnp.bfloat16) for p in in_order(first, new_master, other_master)]
+    params = jnp.concatenate(params, axis=0).reshape(pairs, 1, own, width)
+    bit = shards // 2
+    while bit >= 1:
+        got = swap(params, bit)
+        low = (shard & bit) == 0
+        lo, hi = in_order(low, params, got)
+        params = jnp.stack([lo, hi], axis=2).reshape(pairs, -1, own, width)
+        bit //= 2
+    return (new_master, new_moment, new_second, params.reshape(rows, width))
 
 
 def solution(mesh):

time: 86 us -> 21.7 us (0.25)
  waiting for transfers between devices: 56.7 us -> 6.46 us
  between operations: 14.8 us -> 1.48 us
  blocking collectives: 10 us -> 0 us
  starting transfers between devices: 0.04 us -> 9.18 us
    unnamed x2 -> x0, waiting for transfers between devices: 56.7 us -> none
    all_gather x1 -> x0, blocking collectives: 10 us -> none  [per_device(): params = lax.all_gather(shard_params, ('pair', 'dp'), axis=0, tiled=True)]
    ppermute x0 -> x6, starting transfers between devices: none -> 9.18 us  [swap(): return lax.ppermute(array, GROUP, [(i, i ^ bit) for i in range(size)])]
    ppermute x0 -> x6, waiting for transfers between devices: none -> 6.46 us  [swap(): return lax.ppermute(array, GROUP, [(i, i ^ bit) for i in range(size)])]
    unnamed x1 -> x0, other arithmetic: 2.33 us -> none
    unnamed x10 -> x9, local copies, waits for them, and re-layouts: 1.93 us -> 0.61 us
    convert_element_type x0 -> x2, other arithmetic: none -> 1.08 us  [per_device(): p.astype(jnp.bfloat16)]
    add x0 -> x2, other arithmetic: none -> 0.99 us  [the longest x1 0.96 us: per_device(): local = (local + swap(local, 1)).reshape(pairs, shards, own, width)]
  transfers between devices with their start and end apart: 1 -> 6, of which waited for: 1 -> 5; matrix products, arithmetic and copies ran while one was open for 1% -> 1% of each run, Pallas kernels for 0% -> 0%
where the time goes in v1:
time: 21.7 us; the launch traced here: 21.5 us
  starting transfers between devices  9.18 us (42%)
  waiting for transfers between devices  6.46 us (30%)
  other arithmetic  2.74 us (13%)
  local copies, waits for them, and re-layouts  1.66 us (8%)
  between operations  1.48 us (7%)
    ppermute x6, starting transfers between devices, swap(): return lax.ppermute(array, GROUP, [(i, i ^ bit) for i in range(size)])  9.18 us
    ppermute x6, waiting for transfers between devices, swap(): return lax.ppermute(array, GROUP, [(i, i ^ bit) for i in range(size)])  6.46 us
    convert_element_type x2, other arithmetic, per_device(): p.astype(jnp.bfloat16)  1.08 us
    add x1, other arithmetic, per_device(): local = (local + swap(local, 1)).reshape(pairs, shards, own, width)  0.96 us
    another operation x1, local copies, waits for them, and re-layouts, per_device(): return (new_master, new_moment, new_second, params.reshape(rows, width))  0.7 us
    unnamed x9, local copies, waits for them, and re-layouts  0.61 us
  transfers between devices with their start and end apart: 6, of which 5 were waited for; matrix products, arithmetic and copies ran while one was open for 1% of the time, Pallas kernels for 0%

profile of v1, /device:TPU:0, one launch (start us, length us, event | category | flops | bytes accessed | tf_op | source)
XLA Modules:
  0.0 21.5 jit_solution(14992557900396234186)
XLA Ops:
  0.6 0.5 %collective-permute-start = (f32[8,7168]{1,0:T(8,128)}, f32[8,7168]{1,0:T(8,128)S(1)}, u32[]{:S(2)}, u32[]{:S(2)}) collective-permute-start(f32[8,7168]{1,0:T(8,128)} %bitcast.35), channel_id=1, source_target_pairs={{0,1},{1,0},{2,3},{3,2},{16,17},{17,16},{18,19},{19,18},{4,5},{5,4... | collective-permute-start | bytes 688136 | tf_op jit(solution)/shard_map/ppermute | solution.py:11
  1.1 1.3 %collective-permute-done = f32[8,7168]{1,0:T(8,128)S(1)} collective-permute-done((f32[8,7168]{1,0:T(8,128)}, f32[8,7168]{1,0:T(8,128)S(1)}, u32[]{:S(2)}, u32[]{:S(2)}) %collective-permute-start) | collective-permute-done | bytes 229408 | tf_op jit(solution)/shard_map/ppermute | solution.py:11
  2.5 1.0 %bitcast_add_fusion = f32[8,7168]{1,0:T(8,128)S(1)} fusion(f32[8,7168]{1,0:T(8,128)S(1)} %collective-permute-done, f32[1,1,8,7168]{3,2,1,0:T(8,128)} %param.5), kind=kLoop, calls=%fused_computation.35 | loop fusion | flops 57344 | bytes 688128 | tf_op jit(solution)/shard_map/add | solution.py:43
  3.4 0.1 reshape_reshape.6
  3.6 0.1 constant_dynamic-slice_fusion.1
  3.7 0.0 copy-start
  3.7 0.0 copy-start.1
  3.7 0.0 copy-start.2
  3.8 2.9 %collective-permute-start.1 = (f32[2,1,1,7168]{3,0,2,1:T(2,128)S(1)}, f32[2,1,1,7168]{3,0,2,1:T(2,128)S(1)}, u32[]{:S(2)}, u32[]{:S(2)}) collective-permute-start(f32[2,1,1,7168]{3,0,2,1:T(2,128)S(1)} %bitcast.36), channel_id=1, source_target_pairs={{0,2},{1,3},{2,0},{3,1},{16,18},{17,19},{18,16},{19,17},{4,6},{5,7... | collective-permute-start | bytes 172040 | tf_op jit(solution)/shard_map/ppermute | solution.py:11
  6.7 0.0 copy-done
  6.7 0.0 copy-done.1
  6.7 0.0 copy-done.2
  6.7 0.1 pad_maximum_fusion
  6.8 1.6 %collective-permute-start.3 = (f32[3,7168]{1,0:T(4,128)S(1)}, f32[3,7168]{1,0:T(4,128)S(1)}, u32[]{:S(2)}, u32[]{:S(2)}) collective-permute-start(f32[3,7168]{1,0:T(4,128)S(1)} %pad_maximum_fusion), channel_id=1, source_target_pairs={{0,16},{1,17},{2,18},{3,19},{16,0},{17,1},{18,2},{19,3},{4,20},{5,... | collective-permute-start | bytes 258056 | tf_op jit(solution)/shard_map/ppermute | solution.py:11
  8.4 0.5 %collective-permute-done.1 = f32[2,1,1,7168]{3,0,2,1:T(2,128)S(1)} collective-permute-done((f32[2,1,1,7168]{3,0,2,1:T(2,128)S(1)}, f32[2,1,1,7168]{3,0,2,1:T(2,128)S(1)}, u32[]{:S(2)}, u32[]{:S(2)}) %collective-permute-start.1) | collective-permute-done | bytes 57376 | tf_op jit(solution)/shard_map/ppermute | solution.py:11
  9.0 2.1 %collective-permute-start.2 = (f32[2,7168]{1,0:T(2,128)S(1)}, f32[2,7168]{1,0:T(2,128)S(1)}, u32[]{:S(2)}, u32[]{:S(2)}) collective-permute-start(f32[2,7168]{1,0:T(2,128)S(1)} %fusion.3), channel_id=1, source_target_pairs={{0,16},{1,17},{2,18},{3,19},{16,0},{17,1},{18,2},{19,3},{4,20},{5,... | collective-permute-start | bytes 172040 | tf_op jit(solution)/shard_map/ppermute | solution.py:11
  11.8 1.5 %collective-permute-done.2 = f32[2,7168]{1,0:T(2,128)S(1)} collective-permute-done((f32[2,7168]{1,0:T(2,128)S(1)}, f32[2,7168]{1,0:T(2,128)S(1)}, u32[]{:S(2)}, u32[]{:S(2)}) %collective-permute-start.2) | collective-permute-done | bytes 57376 | tf_op jit(solution)/shard_map/ppermute | solution.py:11
  13.3 0.0 collective-permute-done.3
  13.3 1.0 %fusion.6 = (bf16[1,7168]{1,0:T(2,128)(2,1)S(1)}, bf16[1,7168]{1,0:T(2,128)(2,1)S(1)}, f32[1,7168]{1,0:T(1,128)S(1)}, f32[1,7168]{1,0:T(1,128)}, f32[1,7168]{1,0:T(1,128)}) fusion(pred[]{:T(512)S(6)} %eq.9, f32[]{:T(128)} %bitcast.5, f32[3,7168]{1,0:T(4,128)S(1)} %collective-permute-done.3, f32[]{:T(128)} %bitcast.4, f32[2,7168]{1,0:T(2,128)S(1)} %add.55, ...), kind=kLoop, calls=%fused_computation.21 | loop fusion | flops 243712 | bytes 344073 | tf_op jit(solution)/shard_map/convert_element_type | solution.py:61
  14.3 0.0 copy-start.3
  14.3 0.6 %copy-done.3 = f32[1,7168]{1,0:T(1,128)} copy-done((f32[1,7168]{1,0:T(1,128)}, f32[1,7168]{1,0:T(1,128)S(1)}, u32[]{:S(2)}) %copy-start.3) | copy-done | bytes 28696
  14.9 0.1 maximum_bitcast_fusion.1
  15.0 2.0 %collective-permute-start.4 = (bf16[2,1,1,7168]{3,0,2,1:T(2,128)(2,1)S(1)}, bf16[2,1,1,7168]{3,0,2,1:T(2,128)(2,1)S(1)}, u32[]{:S(2)}, u32[]{:S(2)}) collective-permute-start(bf16[2,1,1,7168]{3,0,2,1:T(2,128)(2,1)S(1)} %maximum_bitcast_fusion.1), channel_id=1, source_target_pairs={{0,2},{1,3},{2,0},{3,1},{16,18},{17,19},{18,16},{19,17},{4,6},{5,7... | collective-permute-start | bytes 86024 | tf_op jit(solution)/shard_map/ppermute | solution.py:11
  17.0 1.9 %collective-permute-done.4 = bf16[2,1,1,7168]{3,0,2,1:T(2,128)(2,1)S(1)} collective-permute-done((bf16[2,1,1,7168]{3,0,2,1:T(2,128)(2,1)S(1)}, bf16[2,1,1,7168]{3,0,2,1:T(2,128)(2,1)S(1)}, u32[]{:S(2)}, u32[]{:S(2)}) %collective-permute-start.4) | collective-permute-done | bytes 28704 | tf_op jit(solution)/shard_map/ppermute | solution.py:11
  18.9 0.1 fusion.8
  19.0 0.1 maximum_bitcast_fusion
  19.1 0.1 collective-permute-start.5
  19.2 1.2 %collective-permute-done.5 = bf16[2,2,1,7168]{3,0,1,2:T(2,128)(2,1)S(1)} collective-permute-done((bf16[2,2,1,7168]{3,0,1,2:T(2,128)(2,1)S(1)}, bf16[2,2,1,7168]{3,0,1,2:T(2,128)(2,1)S(1)}, u32[]{:S(2)}, u32[]{:S(2)}) %collective-permute-start.5) | collective-permute-done | bytes 57376 | tf_op jit(solution)/shard_map/ppermute | solution.py:11
  20.4 0.1 fusion
  20.6 0.2 pad_maximum_fusion.1
  20.7 0.1 copy.11
  20.8 0.7 %reshape_reshape.7 = bf16[8,7168]{1,0:T(8,128)(2,1)} reshape(bf16[2,2,2,1,7168]{4,2,1,0,3:T(2,128)(2,1)S(1)} %copy.11) | data formatting | bytes 229376 | tf_op jit(solution)/shard_map/reshape;reshape | solution.py:70
  (4 shorter events, 0.1 us)
Async XLA Ops:
  0.6 1.8 %collective-permute-start = (f32[8,7168]{1,0:T(8,128)}, f32[8,7168]{1,0:T(8,128)S(1)}, u32[]{:S(2)}, u32[]{:S(2)}) collective-permute-start(f32[8,7168]{1,0:T(8,128)} %bitcast.35), channel_id=1, source_target_pairs={{0,1},{1,0},{2,3},{3,2},{16,17},{17,16},{18,19},{19,18},{4,5},{5,4... | collective-permute-start | bytes 688136 | tf_op jit(solution)/shard_map/ppermute | solution.py:11
  3.7 3.0 %copy-start = (f32[1,7168]{1,0:T(1,128)S(1)}, f32[1,7168]{1,0:T(1,128)}, u32[]{:S(2)}) copy-start(f32[1,7168]{1,0:T(1,128)} %param.8) | copy-start | bytes 86020
  3.7 3.0 %copy-start.1 = (f32[1,7168]{1,0:T(1,128)S(1)}, f32[1,7168]{1,0:T(1,128)}, u32[]{:S(2)}) copy-start(f32[1,7168]{1,0:T(1,128)} %param.7) | copy-start | bytes 86020
  3.7 3.0 %copy-start.2 = (f32[1,7168]{1,0:T(1,128)S(1)}, f32[1,7168]{1,0:T(1,128)}, u32[]{:S(2)}) copy-start(f32[1,7168]{1,0:T(1,128)} %param.6) | copy-start | bytes 86020
  3.8 5.1 %collective-permute-start.1 = (f32[2,1,1,7168]{3,0,2,1:T(2,128)S(1)}, f32[2,1,1,7168]{3,0,2,1:T(2,128)S(1)}, u32[]{:S(2)}, u32[]{:S(2)}) collective-permute-start(f32[2,1,1,7168]{3,0,2,1:T(2,128)S(1)} %bitcast.36), channel_id=1, source_target_pairs={{0,2},{1,3},{2,0},{3,1},{16,18},{17,19},{18,16},{19,17},{4,6},{5,7... | collective-permute-start | bytes 172040 | tf_op jit(solution)/shard_map/ppermute | solution.py:11
  6.8 6.5 %collective-permute-start.3 = (f32[3,7168]{1,0:T(4,128)S(1)}, f32[3,7168]{1,0:T(4,128)S(1)}, u32[]{:S(2)}, u32[]{:S(2)}) collective-permute-start(f32[3,7168]{1,0:T(4,128)S(1)} %pad_maximum_fusion), channel_id=1, source_target_pairs={{0,16},{1,17},{2,18},{3,19},{16,0},{17,1},{18,2},{19,3},{4,20},{5,... | collective-permute-start | bytes 258056 | tf_op jit(solution)/shard_map/ppermute | solution.py:11
  9.0 4.2 %collective-permute-start.2 = (f32[2,7168]{1,0:T(2,128)S(1)}, f32[2,7168]{1,0:T(2,128)S(1)}, u32[]{:S(2)}, u32[]{:S(2)}) collective-permute-start(f32[2,7168]{1,0:T(2,128)S(1)} %fusion.3), channel_id=1, source_target_pairs={{0,16},{1,17},{2,18},{3,19},{16,0},{17,1},{18,2},{19,3},{4,20},{5,... | collective-permute-start | bytes 172040 | tf_op jit(solution)/shard_map/ppermute | solution.py:11
  14.3 0.6 %copy-start.3 = (f32[1,7168]{1,0:T(1,128)}, f32[1,7168]{1,0:T(1,128)S(1)}, u32[]{:S(2)}) copy-start(f32[1,7168]{1,0:T(1,128)S(1)} %get-tuple-element.6) | copy-start | bytes 86020
  15.0 3.9 %collective-permute-start.4 = (bf16[2,1,1,7168]{3,0,2,1:T(2,128)(2,1)S(1)}, bf16[2,1,1,7168]{3,0,2,1:T(2,128)(2,1)S(1)}, u32[]{:S(2)}, u32[]{:S(2)}) collective-permute-start(bf16[2,1,1,7168]{3,0,2,1:T(2,128)(2,1)S(1)} %maximum_bitcast_fusion.1), channel_id=1, source_target_pairs={{0,2},{1,3},{2,0},{3,1},{16,18},{17,19},{18,16},{19,17},{4,6},{5,7... | collective-permute-start | bytes 86024 | tf_op jit(solution)/shard_map/ppermute | solution.py:11
  19.1 1.3 %collective-permute-start.5 = (bf16[2,2,1,7168]{3,0,1,2:T(2,128)(2,1)S(1)}, bf16[2,2,1,7168]{3,0,1,2:T(2,128)(2,1)S(1)}, u32[]{:S(2)}, u32[]{:S(2)}) collective-permute-start(bf16[2,2,1,7168]{3,0,1,2:T(2,128)(2,1)S(1)} %maximum_bitcast_fusion), channel_id=1, source_target_pairs={{0,1},{1,0},{2,3},{3,2},{16,17},{17,16},{18,19},{19,18},{4,5},{5,4... | collective-permute-start | bytes 172040 | tf_op jit(solution)/shard_map/ppermute | solution.py:11
